TPU v7x, 32 devices: a whole 2x2x4 slice. The times are simulated.
32 devices in a mesh: groups: 2 (over y), beam: 4 (over z), angle: 2 (over core), trans: 2 (over x).
Axes of the slice: x: 2, y: 2, z: 4, core: 2. Of those that a mesh axis runs over, the one named last changes fastest.
Arguments:
- density: float32 [4, 8, 128, 512], P(None, 'groups', 'beam', 'trans'), parts along dimension 1, may hold values from 0.2 to 1.5
- measured: float32 [4, 8, 4, 512], P('angle', 'groups', None, 'trans'), parts along dimension 1, may hold values from -3 to 3
- offsets: int32 [4], P('angle'), may hold values from -4 to 3, as said below
- sides: int32 [4], P('angle'), may hold values from 0 to 1, as said below
- shear_frac: float32 [4], P('angle'), may hold values from 0.1 to 0.9
- k_incident: float32 [4], replicated, may hold values from 0.5 to 3
- k_fluor: float32 [4, 4], replicated, may hold values from 0.2 to 2
Outputs:
- updated: float32 [4, 8, 128, 512], P(None, ('groups', 'angle'), 'beam', 'trans'), parts along dimension 1
- residual: float32 [4, 8, 4, 512], P('angle', 'groups', None, 'trans'), parts along dimension 1
There are 2 independent parts, one for each index of `groups`. A program takes and returns all parts, laid end to end along the dimension named above; an argument that names none is the same for every part. Nothing has to cross between parts.
Inputs may be any that keep to these rules, and one draw needn't show every extreme that they name: `offsets`: each offset lies in -4 to 3, and both ends occur among the angles. `sides`: exactly half of the angles, rounded down, have detector side 1.
All inputs are finite; a program needn't handle non-finite values.
Results may differ from a plain program's by a relative error of at most 0.0003.
Values sent between devices are 32-bit elements; how exact they have to be, the bound alone decides.
A program may use at most 64 MiB of HBM per device.

v0:
```python
import functools

import jax
import jax.numpy as jnp
from jax import lax
from jax.experimental import pallas as pl
from jax.experimental.pallas import tpu as pltpu
from jax.sharding import PartitionSpec as P

F32 = jnp.float32
BF16 = jnp.bfloat16
FAR = 1 << 20
HALO = 4
ROWS = 8


def split(x):
    hi = x.astype(BF16)
    return hi, (x - hi.astype(F32)).astype(BF16)


def nn(a, b):
    return lax.dot_general(a, b, (((1,), (0,)), ((), ())), preferred_element_type=F32)


def nt(a, b):
    return lax.dot_general(a, b, (((1,), (1,)), ((), ())), preferred_element_type=F32)


def iota(shape, dim):
    return lax.broadcasted_iota(jnp.int32, shape, dim)


def two_taps(at_zero, at_one, frac):
    keep = jnp.full((1, at_zero.shape[1]), 1.0 - frac, F32)
    take = jnp.full((1, at_zero.shape[1]), frac, F32)
    keep_hi = keep.astype(BF16).astype(F32)
    take_hi = take.astype(BF16).astype(F32)
    hi = jnp.where(at_zero, keep_hi, jnp.where(at_one, take_hi, 0.0))
    lo = jnp.where(at_zero, keep - keep_hi, jnp.where(at_one, take - take_hi, 0.0))
    return hi.astype(BF16), lo.astype(BF16)


def stack_t(x):
    hi = x.astype(BF16).astype(F32)
    rows = x.shape[0]
    full = -(-3 * rows // 128) * 128
    parts = [hi, x - hi, hi]
    if full > 3 * rows:
        parts.append(jnp.zeros((full - 3 * rows, x.shape[1]), F32))
    return jnp.transpose(jnp.concatenate(parts, axis=0)).astype(BF16)


def stack_w(hi, lo):
    rows = hi.shape[0]
    full = -(-3 * rows // 128) * 128
    parts = [hi.astype(F32), hi.astype(F32), lo.astype(F32)]
    if full > 3 * rows:
        parts.append(jnp.zeros((full - 3 * rows, hi.shape[1]), F32))
    return jnp.concatenate(parts, axis=0).astype(BF16)


def kernel(sizes, dens, meas, offs, sides, fracs, kinc, kfl, upd, res,
           gsend, gbuf, kbuf, pbuf, pabuf, wt, wsd, rsend, rbuf, gmain, mrecv,
           m_hi, m_lo, tri, gs_s, gr_s, ks_s, kr_s, ps_s, pr_s, as_s, ar_s, ms_s, mr_s, rs_s, rr_s):
    nb, na, nx = sizes
    elems, slices, cells, width = dens.shape
    angles = meas.shape[0]
    share = slices // na
    unit = share * cells
    rows_h = elems * unit
    beam_total = cells * nb
    trans_total = width * nx
    dxb = 0.5 / beam_total
    dxt = 0.5 / trans_total
    half = width // 2
    grp = lax.axis_index("groups")
    me_b = lax.axis_index("beam")
    me_a = lax.axis_index("angle")
    me_x = lax.axis_index("trans")

    def dev(b, a, x):
        return (grp, b, a, x)

    def peers(me, count):
        return [lax.rem(me + k, count) for k in range(1, count)]

    barrier = pltpu.get_barrier_semaphore()
    greeted = 0
    for kb in range(nb):
        for kx in range(nx):
            if kb or kx:
                pl.semaphore_signal(barrier, inc=1, device_id_type=pl.DeviceIdType.MESH,
                                    device_id=dev(lax.rem(me_b + kb, nb), me_a, lax.rem(me_x + kx, nx)))
                greeted += 1
    for ka in range(1, na):
        for kx in range(nx):
            pl.semaphore_signal(barrier, inc=1, device_id_type=pl.DeviceIdType.MESH,
                                device_id=dev(me_b, lax.rem(me_a + ka, na), lax.rem(me_x + kx, nx)))
            greeted += 1

    def send(src, dst, ssem, rsem, to):
        copy = pltpu.make_async_remote_copy(src_ref=src, dst_ref=dst, send_sem=ssem, recv_sem=rsem,
                                            device_id=to, device_id_type=pl.DeviceIdType.MESH)
        copy.start()
        return copy

    def arrive(dst, ssem, rsem):
        pltpu.make_async_remote_copy(src_ref=dst, dst_ref=dst, send_sem=ssem, recv_sem=rsem,
                                     device_id=dev(me_b, me_a, me_x),
                                     device_id_type=pl.DeviceIdType.MESH).wait_recv()

    sent = []
    off = [offs[a] for a in range(angles)]
    side = [sides[a] for a in range(angles)]
    frac = [fracs[a] for a in range(angles)]

    def dens_rows(h, e):
        return dens[e, pl.ds(h * share, share)].reshape(unit, width)

    q = iota((2 * ROWS, width), 0)
    u = iota((2 * ROWS, width), 1)
    up = q < ROWS
    qq = jnp.where(up, q, q - ROWS)
    pick = jnp.where((qq < HALO) & (jnp.where(up, width - HALO + qq, qq) == u), 1.0, 0.0)
    e_hi, e_lo = pick.astype(BF16).astype(F32), jnp.zeros_like(pick)

    def counted(t):
        inside = (t + me_x * width >= 0) & (t + me_x * width < trans_total)
        kept = jnp.where(up, t, width - 1 - t) < width
        return kept & inside, jnp.logical_not(kept) & inside

    for a in range(angles):
        t0 = u - off[a]
        in0, out0 = counted(t0)
        in1, out1 = counted(t0 - 1)
        keep = jnp.full((1, width), 1.0 - frac[a], F32)
        take = jnp.full((1, width), frac[a], F32)
        val_in = jnp.where(in0, keep, 0.0) + jnp.where(in1, take, 0.0)
        val_out = jnp.where(out0, keep, 0.0) + jnp.where(out1, take, 0.0)
        val = jnp.where(qq == HALO + a, val_in, jnp.where(qq == HALO + angles + a, val_out, 0.0))
        val_hi = val.astype(BF16).astype(F32)
        e_hi = e_hi + val_hi
        e_lo = e_lo + (val - val_hi)
    e_both = jnp.concatenate([e_hi, e_lo], axis=0).astype(BF16)
    e_hi = e_hi.astype(BF16)

    total = sum(kinc[e] * dens[e] for e in range(elems))
    ksum = jnp.sum(total, axis=1)
    k8 = jnp.concatenate([ksum[:, :half], ksum[:, half:]], axis=0)
    kbuf[me_b * nx + me_x] = k8
    dhl = []
    for h in range(na):
        d = jnp.concatenate([dens_rows(h, e) for e in range(elems)], axis=0)
        d_hi, d_lo = split(d)
        dhl.append((d_hi, d_lo))
        first = nt(e_both, d_hi)
        msg = first[: 2 * ROWS] + first[2 * ROWS :] + nt(e_hi, d_lo)
        gsend[:, h * rows_h : (h + 1) * rows_h] = msg
    prm = iota((ROWS, 128), 0)
    tile = jnp.zeros((ROWS, 128), F32)
    for a in range(angles):
        tile = jnp.where(prm == 3 * a, off[a].astype(F32), tile)
        tile = jnp.where(prm == 3 * a + 1, frac[a], tile)
        tile = jnp.where(prm == 3 * a + 2, side[a].astype(F32), tile)
    pabuf[me_a] = tile

    pl.semaphore_wait(barrier, greeted)
    for x in peers(me_x, nx):
        part = pl.multiple_of(jnp.where(x > me_x, 0, ROWS), ROWS)
        sent.append(send(gsend.at[pl.ds(part, ROWS)], gbuf.at[me_x], gs_s.at[x], gr_s.at[me_x], dev(me_b, me_a, x)))
    for kb in range(1, nb):
        for kx in range(nx):
            b, x = lax.rem(me_b + kb, nb), lax.rem(me_x + kx, nx)
            own = kbuf.at[me_b * nx + me_x]
            sent.append(send(own, own, ks_s.at[b * nx + x], kr_s.at[me_b * nx + me_x], dev(b, me_a, x)))
    for a in peers(me_a, na):
        own = pabuf.at[me_a]
        sent.append(send(own, own, as_s.at[a], ar_s.at[me_a], dev(me_b, a, me_x)))

    k = iota((width + 128, width), 0)
    t = iota((width + 128, width), 1)
    col = jnp.where(k < width + 64, k, k - width - 128)
    d0 = col - t
    td = iota((width, width), 0) - iota((width, width), 1)
    for a in range(angles):
        hi, lo = two_taps(d0 == off[a], d0 == off[a] + 1, frac[a])
        m_hi[a] = hi
        m_lo[a] = lo
        sgn = jnp.where(side[a] == 1, 1, -1)
        tri[a] = jnp.where(td == 0, 0.5, jnp.where(td * sgn > 0, 1.0, 0.0)).astype(BF16)
    r0 = iota((unit, unit), 0)
    r1 = iota((unit, unit), 1)
    same = (r0 // cells) == (r1 // cells)
    low = jnp.where(r0 == r1, 0.5, jnp.where(same & (r1 < r0), 1.0, 0.0)).astype(BF16)
    high = jnp.where(r0 == r1, 0.5, jnp.where(same & (r1 > r0), 1.0, 0.0)).astype(BF16)
    g = iota((ROWS * nx, width), 0)
    gt = iota((ROWS * nx, width), 1)
    gx = g // ROWS
    gq = g - gx * ROWS
    gcol = jnp.where(gx == me_x + 1, width + gq, jnp.where(gx == me_x - 1, gq - HALO, FAR))
    gcol = jnp.where(gq < HALO, gcol, FAR)
    halo_w = []
    for a in range(angles):
        hi, lo = two_taps(gcol - gt == off[a], gcol - gt == off[a] + 1, frac[a])
        seen = jnp.where(side[a] == 1, gx - me_x, me_x - gx)
        use = ((gq == HALO + a) & (seen > 0)) | ((gq == HALO + angles + a) & ((seen == 0) | (seen > 1)))
        ca = jnp.where(use, 1.0, 0.0).astype(BF16)
        halo_w.append((stack_w(hi, lo), stack_w(ca, jnp.zeros_like(ca))))

    sheared0 = [[nn(dhl[h][0], m_hi[a, :width]) + nn(dhl[h][1], m_hi[a, :width]) + nn(dhl[h][0], m_lo[a, :width])
                 for a in range(angles)] for h in range(na)]

    spill = gsend[...]
    own_slot = spill[:ROWS]
    sq = iota((ROWS, spill.shape[1]), 0)
    for a in range(angles):
        pick_up = jnp.where(side[a] == 1, 1, 0)
        chosen = jnp.where((sq == HALO + angles + a) & (pick_up == 0), spill[ROWS:], own_slot)
        own_slot = chosen
    gbuf[me_x] = own_slot

    for x in peers(me_x, nx):
        arrive(gbuf.at[x], gs_s.at[x], gr_s.at[x])
    for kb in range(1, nb):
        for kx in range(nx):
            i = lax.rem(me_b + kb, nb) * nx + lax.rem(me_x + kx, nx)
            arrive(kbuf.at[i], ks_s.at[i], kr_s.at[i])

    ups = []
    for x in range(nx):
        acc = jnp.zeros((2 * slices, half), F32)
        for b in range(nb):
            acc = acc + jnp.where(b < me_b, kbuf[b * nx + x], 0.0)
        ups.append(acc)
    own_up = sum(jnp.where(me_x == x, ups[x], 0.0) for x in range(nx))
    right = sum(jnp.where(me_x + 1 == x, ups[x], 0.0) for x in range(nx))
    left = sum(jnp.where(me_x - 1 == x, ups[x], 0.0) for x in range(nx))
    lane = iota((slices, half), 1)
    rim = jnp.where(lane < 64, right[:slices], left[slices:])
    kext = jnp.concatenate([own_up[:slices], own_up[slices:], rim], axis=1)
    kext = jnp.concatenate([kext, jnp.zeros_like(kext)], axis=0)
    k_hi, k_lo = split(kext)
    carried = [nn(k_hi, m_hi[a]) + nn(k_lo, m_hi[a]) + nn(k_hi, m_lo[a]) for a in range(angles)]

    gall = jnp.concatenate([gbuf[x] for x in range(nx)], axis=0)
    g_t = stack_t(gall)

    def spread_rows(rows):
        return jnp.broadcast_to(rows[:, None, :], (share, cells, width)).reshape(unit, width)

    for h in range(na):
        gh = g_t[h * rows_h : (h + 1) * rows_h]
        for a in range(angles):
            x = sheared0[h][a] + nn(gh, halo_w[a][0])
            x_hi, x_lo = split(x)
            raw = nn(x_hi, tri[a]) + nn(x_lo, tri[a]) + nn(gh, halo_w[a][1])
            atten = sum(kinc[e] * x[e * unit : (e + 1) * unit] for e in range(elems))
            a_hi, a_lo = split(atten)
            inc = dxb * (nn(low, a_hi) + nn(low, a_lo) + spread_rows(carried[a][h * share : (h + 1) * share]))
            for e in range(elems):
                path = inc
                for f in range(elems):
                    path = path + (dxt * kfl[e, f]) * raw[f * unit : (f + 1) * unit]
                w = dxb * jnp.exp(-path)
                ws = w * x[e * unit : (e + 1) * unit]
                wt[h, a, e] = w
                wsd[h, a, e] = ws
                part = jnp.sum(ws.reshape(share, cells, width), axis=1)
                for s in range(share):
                    row = (a * share + s) * elems + e
                    pbuf[me_b, h, row : row + 1] = part[s : s + 1]
        for b in peers(me_b, nb):
            own = pbuf.at[me_b, h]
            sent.append(send(own, own, ps_s.at[h * nb + b], pr_s.at[h * nb + me_b], dev(b, me_a, me_x)))

    for a in peers(me_a, na):
        arrive(pabuf.at[a], as_s.at[a], ar_s.at[a])
    rq = iota((2 * ROWS, width), 0)
    rt = iota((2 * ROWS, width), 1)
    rcol = jnp.where(rq < HALO, width + rq, jnp.where((rq >= ROWS) & (rq < ROWS + HALO), rq - ROWS - HALO, FAR))
    rim_w, sum_w = [], []
    for a in range(angles):
        hi, lo = two_taps(rcol - rt == off[a], rcol - rt == off[a] + 1, frac[a])
        rim_w.append((jnp.concatenate([hi.astype(F32), lo.astype(F32)], axis=0).astype(BF16), hi))
        sum_w.append(jnp.where((rq == HALO + a) | (rq == ROWS + HALO + a), 1.0, 0.0).astype(BF16))

    wq = iota((ROWS, width), 0)
    wu = iota((ROWS, width), 1)
    w_hi, w_lo = [], []
    for x in range(nx):
        for al in range(na):
            place = jnp.where(me_x == x + 1, wq, jnp.where(me_x == x - 1, width - HALO + wq, FAR))
            val = jnp.where((wq < HALO) & (place == wu), 1.0, 0.0)
            for a in range(angles):
                o = pabuf[al, 3 * a : 3 * a + 1, 0:1]
                fr = pabuf[al, 3 * a + 1 : 3 * a + 2, 0:1]
                sd = pabuf[al, 3 * a + 2 : 3 * a + 3, 0:1]
                t0 = (wu + me_x * width).astype(F32) - o

                def sees(tt):
                    above = (tt >= (x + 1) * width) & (tt < trans_total)
                    below = (tt < x * width) & (tt >= 0)
                    return jnp.where(sd > 0.5, jnp.where(above, 1.0, 0.0), jnp.where(below, 1.0, 0.0))

                both = (1.0 - fr) * sees(t0) + fr * sees(t0 - 1.0)
                val = jnp.where(wq == HALO + a, both, val)
            hi = val.astype(BF16).astype(F32)
            w_hi.append(hi)
            w_lo.append(val - hi)
    fold_w = stack_w(jnp.concatenate(w_hi, axis=0), jnp.concatenate(w_lo, axis=0))

    for kh in range(na):
        h = lax.rem(me_a + 1 + kh, na)
        for b in peers(me_b, nb):
            arrive(pbuf.at[b, h], ps_s.at[h * nb + b], pr_s.at[h * nb + b])
        full = pbuf[0, h]
        down = jnp.where(0 > me_b, full, 0.0)
        for b in range(1, nb):
            full = full + pbuf[b, h]
            down = down + jnp.where(b > me_b, pbuf[b, h], 0.0)
        missed = []
        for a in range(angles):
            for s in range(share):
                row = (a * share + s) * elems
                m = full[row : row + elems] - meas[a, h * share + s]
                res[a, h * share + s] = m
                missed.append(m)
        m_all = jnp.concatenate(missed, axis=0)
        later_all = m_all * down
        gext = None
        msg = None
        for a in range(angles):
            def per_slice(rows_of):
                return jnp.concatenate(
                    [jnp.broadcast_to(rows_of(s), (cells, width)) for s in range(share)], axis=0)

            later = per_slice(lambda s: jnp.sum(
                later_all[(a * share + s) * elems : (a * share + s + 1) * elems], axis=0, keepdims=True))
            direct, prod = [], []
            for e in range(elems):
                me = per_slice(lambda s: m_all[(a * share + s) * elems + e : (a * share + s) * elems + e + 1])
                direct.append(me * wt[h, a, e])
                prod.append(me * wsd[h, a, e])
            s_hi, s_lo = split(sum(prod))
            ga = -dxb * (nn(high, s_hi) + nn(high, s_lo) + later)
            mix = jnp.concatenate(
                [sum((-dxt * kfl[e, f]) * prod[e] for e in range(elems)) for f in range(elems)], axis=0)
            x_hi, x_lo = split(mix)
            back = nt(x_hi, tri[a]) + nt(x_lo, tri[a])
            gs = jnp.concatenate(
                [direct[f] + kinc[f] * ga + back[f * unit : (f + 1) * unit] for f in range(elems)], axis=0)
            g_hi, g_lo = split(gs)
            own = (slice(0, width), slice(None))
            term = nt(g_hi, m_hi[a, :width]) + nt(g_lo, m_hi[a, :width]) + nt(g_hi, m_lo[a, :width])
            gext = term if gext is None else gext + term
            first = nt(rim_w[a][0], g_hi)
            mm = first[: 2 * ROWS] + first[2 * ROWS :] + nt(rim_w[a][1], g_lo)
            mm = mm + nt(sum_w[a], x_hi) + nt(sum_w[a], x_lo)
            msg = mm if msg is None else msg + mm
        gmain[h] = gext
        rsend[h] = msg
        if kh < na - 1:
            sent.append(send(gmain.at[h], mrecv.at[me_a], ms_s.at[h], mr_s.at[me_a], dev(me_b, h, me_x)))
        for kx in range(nx):
            x = lax.rem(me_x + kx, nx)
            if kx == 0 and kh == na - 1:
                continue
            part = pl.multiple_of(jnp.where(x >= me_x, 0, ROWS), ROWS)
            slot = me_x * na + me_a
            sent.append(send(rsend.at[h, pl.ds(part, ROWS)], rbuf.at[slot], rs_s.at[h * nx + x], rr_s.at[slot], dev(me_b, h, x)))
    rbuf[me_x * na + me_a] = rsend[me_a, :ROWS]

    total = gmain[me_a]
    for a in peers(me_a, na):
        arrive(mrecv.at[a], ms_s.at[a], mr_s.at[a])
        total = total + mrecv[a]
    for ka in range(na):
        for kx in range(nx):
            if ka or kx:
                i = lax.rem(me_x + kx, nx) * na + lax.rem(me_a + ka, na)
                arrive(rbuf.at[i], rs_s.at[0], rr_s.at[i])
    rall = jnp.concatenate([rbuf[i] for i in range(nx * na)], axis=0)
    total = total + nn(stack_t(rall), fold_w)
    step = 8.0 * beam_total / (angles * na)
    for f in range(elems):
        new = dens[f, pl.ds(me_a * share, share)].reshape(unit, width) - step * total[f * unit : (f + 1) * unit]
        upd[f] = new.reshape(share, cells, width)
    for copy in sent:
        copy.wait_send()


def local(sizes, density, measured, offsets, sides, shear_frac, k_incident, k_fluor):
    nb, na, nx = sizes
    elems, slices, cells, width = density.shape
    angles = measured.shape[0]
    share = slices // na
    unit = share * cells
    rows_h = elems * unit
    vm = pl.BlockSpec(memory_space=pltpu.VMEM)
    sm = pl.BlockSpec(memory_space=pltpu.SMEM)
    dma = pltpu.SemaphoreType.DMA
    return pl.pallas_call(
        functools.partial(kernel, sizes),
        out_shape=(
            jax.ShapeDtypeStruct((elems, share, cells, width), F32),
            jax.ShapeDtypeStruct(measured.shape, F32),
        ),
        in_specs=[vm, vm, sm, sm, sm, sm, sm],
        out_specs=(vm, vm),
        scratch_shapes=[
            pltpu.VMEM((2 * ROWS, na * rows_h), F32),
            pltpu.VMEM((nx, ROWS, na * rows_h), F32),
            pltpu.VMEM((nb * nx, 2 * slices, width // 2), F32),
            pltpu.VMEM((nb, na, angles * share * elems, width), F32),
            pltpu.VMEM((na, ROWS, 128), F32),
            pltpu.VMEM((na, angles, elems, unit, width), F32),
            pltpu.VMEM((na, angles, elems, unit, width), F32),
            pltpu.VMEM((na, 2 * ROWS, rows_h), F32),
            pltpu.VMEM((nx * na, ROWS, rows_h), F32),
            pltpu.VMEM((na, rows_h, width), F32),
            pltpu.VMEM((na, rows_h, width), F32),
            pltpu.VMEM((angles, width + 128, width), BF16),
            pltpu.VMEM((angles, width + 128, width), BF16),
            pltpu.VMEM((angles, width, width), BF16),
            dma((nx,)), dma((nx,)),
            dma((nb * nx,)), dma((nb * nx,)),
            dma((na * nb,)), dma((na * nb,)),
            dma((na,)), dma((na,)),
            dma((na,)), dma((na,)),
            dma((na * nx,)), dma((na * nx,)),
        ],
        compiler_params=pltpu.CompilerParams(
            collective_id=0, has_side_effects=True, vmem_limit_bytes=40 * 1024 * 1024
        ),
    )(density, measured, offsets, sides, shear_frac, k_incident, k_fluor)


def solution(mesh):
    sizes = (mesh.shape["beam"], mesh.shape["angle"], mesh.shape["trans"])
    return jax.shard_map(
        functools.partial(local, sizes),
        mesh=mesh,
        in_specs=(
            P(None, "groups", "beam", "trans"),
            P("angle", "groups", None, "trans"),
            P("angle"),
            P("angle"),
            P("angle"),
            P(),
            P(),
        ),
        out_specs=(
            P(None, ("groups", "angle"), "beam", "trans"),
            P("angle", "groups", None, "trans"),
        ),
        check_vma=False,
    )
```

profile of v0, /device:TPU:0, one launch (start us, length us, event | category | flops | bytes accessed | tf_op | source)
XLA Modules:
  0.0 29.6 jit_solution(1671280380849878164)
XLA Ops:
  0.6 0.0 copy-start
  0.6 1.0 %copy-done = f32[4,4,32,256]{3,2,1,0:T(8,128)S(1)} copy-done((f32[4,4,32,256]{3,2,1,0:T(8,128)S(1)}, f32[4,4,32,256]{3,2,1,0:T(8,128)}, u32[]{:S(2)}) %copy-start) | copy-done | bytes 524312
  1.7 0.0 copy-start.1
  1.7 0.8 %copy-done.1 = f32[2,4,4,256]{3,2,1,0:T(4,128)S(1)} copy-done((f32[2,4,4,256]{3,2,1,0:T(4,128)S(1)}, f32[2,4,4,256]{3,2,1,0:T(4,128)}, u32[]{:S(2)}) %copy-start.1) | copy-done | bytes 32792
  2.4 0.0 copy-start.2
  2.4 0.7 %copy-done.2 = f32[4,4]{1,0:T(4,128)S(1)} copy-done((f32[4,4]{1,0:T(4,128)S(1)}, f32[4,4]{1,0:T(4,128)}, u32[]{:S(2)}) %copy-start.2) | copy-done | bytes 88
  3.1 0.0 copy-start.3
  3.1 0.7 %copy-done.3 = s32[2]{0:T(128)S(1)} copy-done((s32[2]{0:T(128)S(1)}, s32[2]{0:T(128)}, u32[]{:S(2)}) %copy-start.3) | copy-done | bytes 32
  3.8 0.0 copy-start.4
  3.8 0.7 %copy-done.4 = s32[2]{0:T(128)S(1)} copy-done((s32[2]{0:T(128)S(1)}, s32[2]{0:T(128)}, u32[]{:S(2)}) %copy-start.4) | copy-done | bytes 32
  4.4 0.0 copy-start.5
  4.4 0.7 %copy-done.5 = f32[2]{0:T(128)S(1)} copy-done((f32[2]{0:T(128)S(1)}, f32[2]{0:T(128)}, u32[]{:S(2)}) %copy-start.5) | copy-done | bytes 32
  5.1 0.0 copy-start.6
  5.1 0.7 %copy-done.6 = f32[4]{0:T(128)S(1)} copy-done((f32[4]{0:T(128)S(1)}, f32[4]{0:T(128)}, u32[]{:S(2)}) %copy-start.6) | copy-done | bytes 40
  5.7 22.5 %shard_map.86 = (f32[4,2,32,256]{3,2,1,0:T(8,128)S(1)}, f32[2,4,4,256]{3,2,1,0:T(4,128)S(1)}) custom-call(f32[4,4,32,256]{3,2,1,0:T(8,128)S(1)} %copy-done, f32[2,4,4,256]{3,2,1,0:T(4,128)S(1)} %copy-done.1, s32[2]{0:T(128)S(1)} %copy-done.3, s32[2]{0:T(128)S(1)} %copy-done.4, f32[2]{0:T(128)S(1)} %copy-done.5, f32[4]{0:T(128)S(1)} %copy-done.6, ...), custom_call_target="tpu_custom_call" | custom-call | tf_op jit(solution)/shard_map/pallas_call | solution.py:403
  28.3 0.7 %copy.11 = f32[4,2,32,256]{3,2,1,0:T(8,128)} copy(f32[4,2,32,256]{3,2,1,0:T(8,128)S(1)} %get-tuple-element.4) | data formatting | bytes 524288
  29.0 0.6 %copy.12 = f32[2,4,4,256]{3,2,1,0:T(4,128)} copy(f32[2,4,4,256]{3,2,1,0:T(4,128)S(1)} %get-tuple-element.5) | data formatting | bytes 65536
Async XLA Ops:
  0.6 1.0 %copy-start = (f32[4,4,32,256]{3,2,1,0:T(8,128)S(1)}, f32[4,4,32,256]{3,2,1,0:T(8,128)}, u32[]{:S(2)}) copy-start(f32[4,4,32,256]{3,2,1,0:T(8,128)} %dens.1) | copy-start | bytes 1572868
  1.7 0.8 %copy-start.1 = (f32[2,4,4,256]{3,2,1,0:T(4,128)S(1)}, f32[2,4,4,256]{3,2,1,0:T(4,128)}, u32[]{:S(2)}) copy-start(f32[2,4,4,256]{3,2,1,0:T(4,128)} %meas.1) | copy-start | bytes 98308
  2.4 0.7 %copy-start.2 = (f32[4,4]{1,0:T(4,128)S(1)}, f32[4,4]{1,0:T(4,128)}, u32[]{:S(2)}) copy-start(f32[4,4]{1,0:T(4,128)} %kfl.1) | copy-start | bytes 196
  3.1 0.7 %copy-start.3 = (s32[2]{0:T(128)S(1)}, s32[2]{0:T(128)}, u32[]{:S(2)}) copy-start(s32[2]{0:T(128)} %offs.1) | copy-start | bytes 28
  3.8 0.7 %copy-start.4 = (s32[2]{0:T(128)S(1)}, s32[2]{0:T(128)}, u32[]{:S(2)}) copy-start(s32[2]{0:T(128)} %sides.1) | copy-start | bytes 28
  4.4 0.7 %copy-start.5 = (f32[2]{0:T(128)S(1)}, f32[2]{0:T(128)}, u32[]{:S(2)}) copy-start(f32[2]{0:T(128)} %fracs.1) | copy-start | bytes 28
  5.1 0.7 %copy-start.6 = (f32[4]{0:T(128)S(1)}, f32[4]{0:T(128)}, u32[]{:S(2)}) copy-start(f32[4]{0:T(128)} %kinc.1) | copy-start | bytes 52
where the time goes:
time: 29.9 us; the launch traced here: 29.6 us
  Pallas kernels  22.5 us (75%)
  local copies, waits for them, and re-layouts  6.41 us (21%)
  between operations  0.66 us (2%)
    pallas_call x1, Pallas kernels, local(): pl.pallas_call(functools.partial(kernel, sizes), out_shape=(jax.ShapeDtyp...  22.5 us
    unnamed x16, local copies, waits for them, and re-layouts  6.41 us

commit v1 on v0

--- a/solution.py
+++ b/solution.py
@@ -60,9 +60,16 @@
     return jnp.concatenate(parts, axis=0).astype(BF16)
 
 
-def kernel(sizes, dens, meas, offs, sides, fracs, kinc, kfl, upd, res,
+def kernel(sizes, dens_in, meas_in, offs_in, sides_in, fracs_in, kinc_in, kfl_in, upd_out, res_out,
+           dens, meas, offs, sides, fracs, kinc, kfl, in_s, upd, res, out_s,
            gsend, gbuf, kbuf, pbuf, pabuf, wt, wsd, rsend, rbuf, gmain, mrecv,
-           m_hi, m_lo, tri, gs_s, gr_s, ks_s, kr_s, ps_s, pr_s, as_s, ar_s, ms_s, mr_s, rs_s, rr_s):
+           m_hi, m_lo, car, tri, gs_s, gr_s, ks_s, kr_s, ps_s, pr_s, as_s, ar_s, ms_s, mr_s, rs_s, rr_s):
+    loads = []
+    pairs = ((offs_in, offs), (sides_in, sides), (fracs_in, fracs), (kinc_in, kinc), (kfl_in, kfl),
+             (dens_in, dens), (meas_in, meas))
+    for i, (src, dst) in enumerate(pairs):
+        loads.append(pltpu.make_async_copy(src, dst, in_s.at[i]))
+        loads[-1].start()
     nb, na, nx = sizes
     elems, slices, cells, width = dens.shape
     angles = meas.shape[0]
@@ -110,6 +117,8 @@
                                      device_id=dev(me_b, me_a, me_x),
                                      device_id_type=pl.DeviceIdType.MESH).wait_recv()
 
+    for copy in loads[:5]:
+        copy.wait()
     sent = []
     off = [offs[a] for a in range(angles)]
     side = [sides[a] for a in range(angles)]
@@ -145,18 +154,20 @@
     e_both = jnp.concatenate([e_hi, e_lo], axis=0).astype(BF16)
     e_hi = e_hi.astype(BF16)
 
+    loads[5].wait()
     total = sum(kinc[e] * dens[e] for e in range(elems))
     ksum = jnp.sum(total, axis=1)
     k8 = jnp.concatenate([ksum[:, :half], ksum[:, half:]], axis=0)
     kbuf[me_b * nx + me_x] = k8
     dhl = []
-    for h in range(na):
+    order = [lax.rem(me_a + 1 + kh, na) for kh in range(na)]
+    for h in order:
         d = jnp.concatenate([dens_rows(h, e) for e in range(elems)], axis=0)
         d_hi, d_lo = split(d)
         dhl.append((d_hi, d_lo))
         first = nt(e_both, d_hi)
         msg = first[: 2 * ROWS] + first[2 * ROWS :] + nt(e_hi, d_lo)
-        gsend[:, h * rows_h : (h + 1) * rows_h] = msg
+        gsend[:, pl.ds(pl.multiple_of(h * rows_h, rows_h), rows_h)] = msg
     prm = iota((ROWS, 128), 0)
     tile = jnp.zeros((ROWS, 128), F32)
     for a in range(angles):
@@ -241,23 +252,24 @@
     kext = jnp.concatenate([own_up[:slices], own_up[slices:], rim], axis=1)
     kext = jnp.concatenate([kext, jnp.zeros_like(kext)], axis=0)
     k_hi, k_lo = split(kext)
-    carried = [nn(k_hi, m_hi[a]) + nn(k_lo, m_hi[a]) + nn(k_hi, m_lo[a]) for a in range(angles)]
-
-    gall = jnp.concatenate([gbuf[x] for x in range(nx)], axis=0)
-    g_t = stack_t(gall)
-
-    def spread_rows(rows):
-        return jnp.broadcast_to(rows[:, None, :], (share, cells, width)).reshape(unit, width)
-
-    for h in range(na):
-        gh = g_t[h * rows_h : (h + 1) * rows_h]
+    for a in range(angles):
+        car[a] = nn(k_hi, m_hi[a]) + nn(k_lo, m_hi[a]) + nn(k_hi, m_lo[a])
+
+
+    def spread_rows(a, h):
+        return jnp.concatenate(
+            [jnp.broadcast_to(car[a, pl.ds(h * share + s, 1)], (cells, width)) for s in range(share)], axis=0)
+
+    for kh, h in enumerate(order):
+        cols = pl.ds(pl.multiple_of(h * rows_h, rows_h), rows_h)
+        gh = stack_t(jnp.concatenate([gbuf[x, :, cols] for x in range(nx)], axis=0))
         for a in range(angles):
-            x = sheared0[h][a] + nn(gh, halo_w[a][0])
+            x = sheared0[kh][a] + nn(gh, halo_w[a][0])
             x_hi, x_lo = split(x)
             raw = nn(x_hi, tri[a]) + nn(x_lo, tri[a]) + nn(gh, halo_w[a][1])
             atten = sum(kinc[e] * x[e * unit : (e + 1) * unit] for e in range(elems))
             a_hi, a_lo = split(atten)
-            inc = dxb * (nn(low, a_hi) + nn(low, a_lo) + spread_rows(carried[a][h * share : (h + 1) * share]))
+            inc = dxb * (nn(low, a_hi) + nn(low, a_lo) + spread_rows(a, h))
             for e in range(elems):
                 path = inc
                 for f in range(elems):
@@ -310,8 +322,8 @@
             w_lo.append(val - hi)
     fold_w = stack_w(jnp.concatenate(w_hi, axis=0), jnp.concatenate(w_lo, axis=0))
 
-    for kh in range(na):
-        h = lax.rem(me_a + 1 + kh, na)
+    loads[6].wait()
+    for kh, h in enumerate(order):
         for b in peers(me_b, nb):
             arrive(pbuf.at[b, h], ps_s.at[h * nb + b], pr_s.at[h * nb + b])
         full = pbuf[0, h]
@@ -351,7 +363,6 @@
             gs = jnp.concatenate(
                 [direct[f] + kinc[f] * ga + back[f * unit : (f + 1) * unit] for f in range(elems)], axis=0)
             g_hi, g_lo = split(gs)
-            own = (slice(0, width), slice(None))
             term = nt(g_hi, m_hi[a, :width]) + nt(g_lo, m_hi[a, :width]) + nt(g_hi, m_lo[a, :width])
             gext = term if gext is None else gext + term
             first = nt(rim_w[a][0], g_hi)
@@ -371,6 +382,8 @@
             sent.append(send(rsend.at[h, pl.ds(part, ROWS)], rbuf.at[slot], rs_s.at[h * nx + x], rr_s.at[slot], dev(me_b, h, x)))
     rbuf[me_x * na + me_a] = rsend[me_a, :ROWS]
 
+    stores = [pltpu.make_async_copy(res, res_out, out_s.at[elems])]
+    stores[0].start()
     total = gmain[me_a]
     for a in peers(me_a, na):
         arrive(mrecv.at[a], ms_s.at[a], mr_s.at[a])
@@ -386,8 +399,12 @@
     for f in range(elems):
         new = dens[f, pl.ds(me_a * share, share)].reshape(unit, width) - step * total[f * unit : (f + 1) * unit]
         upd[f] = new.reshape(share, cells, width)
+        stores.append(pltpu.make_async_copy(upd.at[f], upd_out.at[f], out_s.at[f]))
+        stores[-1].start()
     for copy in sent:
         copy.wait_send()
+    for copy in stores:
+        copy.wait()
 
 
 def local(sizes, density, measured, offsets, sides, shear_frac, k_incident, k_fluor):
@@ -397,8 +414,7 @@
     share = slices // na
     unit = share * cells
     rows_h = elems * unit
-    vm = pl.BlockSpec(memory_space=pltpu.VMEM)
-    sm = pl.BlockSpec(memory_space=pltpu.SMEM)
+    hbm = pl.BlockSpec(memory_space=pl.ANY)
     dma = pltpu.SemaphoreType.DMA
     return pl.pallas_call(
         functools.partial(kernel, sizes),
@@ -406,9 +422,20 @@
             jax.ShapeDtypeStruct((elems, share, cells, width), F32),
             jax.ShapeDtypeStruct(measured.shape, F32),
         ),
-        in_specs=[vm, vm, sm, sm, sm, sm, sm],
-        out_specs=(vm, vm),
+        in_specs=[hbm] * 7,
+        out_specs=(hbm, hbm),
         scratch_shapes=[
+            pltpu.VMEM(density.shape, F32),
+            pltpu.VMEM(measured.shape, F32),
+            pltpu.SMEM(offsets.shape, jnp.int32),
+            pltpu.SMEM(sides.shape, jnp.int32),
+            pltpu.SMEM(shear_frac.shape, F32),
+            pltpu.SMEM(k_incident.shape, F32),
+            pltpu.SMEM(k_fluor.shape, F32),
+            dma((7,)),
+            pltpu.VMEM((elems, share, cells, width), F32),
+            pltpu.VMEM(measured.shape, F32),
+            dma((elems + 1,)),
             pltpu.VMEM((2 * ROWS, na * rows_h), F32),
             pltpu.VMEM((nx, ROWS, na * rows_h), F32),
             pltpu.VMEM((nb * nx, 2 * slices, width // 2), F32),
@@ -422,6 +449,7 @@
             pltpu.VMEM((na, rows_h, width), F32),
             pltpu.VMEM((angles, width + 128, width), BF16),
             pltpu.VMEM((angles, width + 128, width), BF16),
+            pltpu.VMEM((angles, 2 * slices, width), F32),
             pltpu.VMEM((angles, width, width), BF16),
             dma((nx,)), dma((nx,)),
             dma((nb * nx,)), dma((nb * nx,)),
@@ -431,7 +459,7 @@
             dma((na * nx,)), dma((na * nx,)),
         ],
         compiler_params=pltpu.CompilerParams(
-            collective_id=0, has_side_effects=True, vmem_limit_bytes=40 * 1024 * 1024
+            collective_id=0, has_side_effects=True, vmem_limit_bytes=64 * 1024 * 1024
         ),
     )(density, measured, offsets, sides, shear_frac, k_incident, k_fluor)
 

time: 29.9 us -> 25 us (0.84)
  local copies, waits for them, and re-layouts: 6.41 us -> 2.3 us
  Pallas kernels: 22.5 us -> 21.9 us
    unnamed x16 -> x4, local copies, waits for them, and re-layouts: 6.41 us -> 2.3 us
    pallas_call x1, Pallas kernels: 22.5 us -> 21.9 us  [local(): pl.pallas_call(functools.partial(kernel, sizes), out_shape=(jax.ShapeDtyp...]
where the time goes in v1:
time: 25 us; the launch traced here: 24.8 us
  Pallas kernels  21.9 us (88%)
  local copies, waits for them, and re-layouts  2.3 us (9%)
  between operations  0.65 us (3%)
    pallas_call x1, Pallas kernels, local(): pl.pallas_call(functools.partial(kernel, sizes), out_shape=(jax.ShapeDtyp...  21.9 us
    unnamed x4, local copies, waits for them, and re-layouts  2.3 us

profile of v1, /device:TPU:0, one launch (start us, length us, event | category | flops | bytes accessed | tf_op | source)
XLA Modules:
  0.0 24.8 jit_solution(13285028142701768975)
XLA Ops:
  0.6 21.9 %shard_map.86 = (f32[4,2,32,256]{3,2,1,0:T(8,128)}, f32[2,4,4,256]{3,2,1,0:T(4,128)}) custom-call(f32[4,4,32,256]{3,2,1,0:T(8,128)} %dens_in.1, f32[2,4,4,256]{3,2,1,0:T(4,128)} %meas_in.1, s32[2]{0:T(128)} %offs_in.1, s32[2]{0:T(128)} %sides_in.1, f32[2]{0:T(128)} %fracs_in.1, f32[4]{0:T(128)} %kinc_in.1, f32[4,4]{1,0:T(4,128)} %kfl_in.1), custom_call_target="tpu_custom_call" | custom-call | tf_op jit(solution)/shard_map/pallas_call | solution.py:419
  22.5 0.0 copy-start
  22.5 1.7 %copy.11 = f32[4,2,32,256]{3,2,1,0:T(8,128)} copy(f32[4,2,32,256]{3,2,1,0:T(8,128)} %get-tuple-element.4) | data formatting | bytes 524288
  24.2 0.0 copy-done
  24.2 0.6 %copy.12 = f32[2,4,4,256]{3,2,1,0:T(4,128)} copy(f32[2,4,4,256]{3,2,1,0:T(4,128)S(1)} %copy-done) | data formatting | bytes 65536
Async XLA Ops:
  22.5 1.7 %copy-start = (f32[2,4,4,256]{3,2,1,0:T(4,128)S(1)}, f32[2,4,4,256]{3,2,1,0:T(4,128)}, u32[]{:S(2)}) copy-start(f32[2,4,4,256]{3,2,1,0:T(4,128)} %get-tuple-element.5) | copy-start | bytes 98308

commit v2 on v1

--- a/solution.py
+++ b/solution.py
@@ -177,14 +177,14 @@
     pabuf[me_a] = tile
 
     pl.semaphore_wait(barrier, greeted)
-    for x in peers(me_x, nx):
-        part = pl.multiple_of(jnp.where(x > me_x, 0, ROWS), ROWS)
-        sent.append(send(gsend.at[pl.ds(part, ROWS)], gbuf.at[me_x], gs_s.at[x], gr_s.at[me_x], dev(me_b, me_a, x)))
     for kb in range(1, nb):
         for kx in range(nx):
             b, x = lax.rem(me_b + kb, nb), lax.rem(me_x + kx, nx)
             own = kbuf.at[me_b * nx + me_x]
             sent.append(send(own, own, ks_s.at[b * nx + x], kr_s.at[me_b * nx + me_x], dev(b, me_a, x)))
+    for x in peers(me_x, nx):
+        part = pl.multiple_of(jnp.where(x > me_x, 0, ROWS), ROWS)
+        sent.append(send(gsend.at[pl.ds(part, ROWS)], gbuf.at[me_x], gs_s.at[x], gr_s.at[me_x], dev(me_b, me_a, x)))
     for a in peers(me_a, na):
         own = pabuf.at[me_a]
         sent.append(send(own, own, as_s.at[a], ar_s.at[me_a], dev(me_b, a, me_x)))
@@ -233,6 +233,22 @@
 
     for x in peers(me_x, nx):
         arrive(gbuf.at[x], gs_s.at[x], gr_s.at[x])
+    def spread_rows(a, h):
+        return jnp.concatenate(
+            [jnp.broadcast_to(car[a, pl.ds(h * share + s, 1)], (cells, width)) for s in range(share)], axis=0)
+
+    early = []
+    for kh, h in enumerate(order):
+        cols = pl.ds(pl.multiple_of(h * rows_h, rows_h), rows_h)
+        gh = stack_t(jnp.concatenate([gbuf[x, :, cols] for x in range(nx)], axis=0))
+        for a in range(angles):
+            x = sheared0[kh][a] + nn(gh, halo_w[a][0])
+            x_hi, x_lo = split(x)
+            raw = nn(x_hi, tri[a]) + nn(x_lo, tri[a]) + nn(gh, halo_w[a][1])
+            atten = sum(kinc[e] * x[e * unit : (e + 1) * unit] for e in range(elems))
+            a_hi, a_lo = split(atten)
+            early.append((x, raw, nn(low, a_hi) + nn(low, a_lo)))
+
     for kb in range(1, nb):
         for kx in range(nx):
             i = lax.rem(me_b + kb, nb) * nx + lax.rem(me_x + kx, nx)
@@ -256,20 +272,10 @@
         car[a] = nn(k_hi, m_hi[a]) + nn(k_lo, m_hi[a]) + nn(k_hi, m_lo[a])
 
 
-    def spread_rows(a, h):
-        return jnp.concatenate(
-            [jnp.broadcast_to(car[a, pl.ds(h * share + s, 1)], (cells, width)) for s in range(share)], axis=0)
-
     for kh, h in enumerate(order):
-        cols = pl.ds(pl.multiple_of(h * rows_h, rows_h), rows_h)
-        gh = stack_t(jnp.concatenate([gbuf[x, :, cols] for x in range(nx)], axis=0))
         for a in range(angles):
-            x = sheared0[kh][a] + nn(gh, halo_w[a][0])
-            x_hi, x_lo = split(x)
-            raw = nn(x_hi, tri[a]) + nn(x_lo, tri[a]) + nn(gh, halo_w[a][1])
-            atten = sum(kinc[e] * x[e * unit : (e + 1) * unit] for e in range(elems))
-            a_hi, a_lo = split(atten)
-            inc = dxb * (nn(low, a_hi) + nn(low, a_lo) + spread_rows(a, h))
+            x, raw, ahead = early[kh * angles + a]
+            inc = dxb * (ahead + spread_rows(a, h))
             for e in range(elems):
                 path = inc
                 for f in range(elems):
@@ -340,7 +346,7 @@
                 missed.append(m)
         m_all = jnp.concatenate(missed, axis=0)
         later_all = m_all * down
-        gext = None
+        halves = []
         msg = None
         for a in range(angles):
             def per_slice(rows_of):
@@ -363,16 +369,12 @@
             gs = jnp.concatenate(
                 [direct[f] + kinc[f] * ga + back[f * unit : (f + 1) * unit] for f in range(elems)], axis=0)
             g_hi, g_lo = split(gs)
-            term = nt(g_hi, m_hi[a, :width]) + nt(g_lo, m_hi[a, :width]) + nt(g_hi, m_lo[a, :width])
-            gext = term if gext is None else gext + term
+            halves.append((g_hi, g_lo))
             first = nt(rim_w[a][0], g_hi)
             mm = first[: 2 * ROWS] + first[2 * ROWS :] + nt(rim_w[a][1], g_lo)
             mm = mm + nt(sum_w[a], x_hi) + nt(sum_w[a], x_lo)
             msg = mm if msg is None else msg + mm
-        gmain[h] = gext
         rsend[h] = msg
-        if kh < na - 1:
-            sent.append(send(gmain.at[h], mrecv.at[me_a], ms_s.at[h], mr_s.at[me_a], dev(me_b, h, me_x)))
         for kx in range(nx):
             x = lax.rem(me_x + kx, nx)
             if kx == 0 and kh == na - 1:
@@ -380,6 +382,11 @@
             part = pl.multiple_of(jnp.where(x >= me_x, 0, ROWS), ROWS)
             slot = me_x * na + me_a
             sent.append(send(rsend.at[h, pl.ds(part, ROWS)], rbuf.at[slot], rs_s.at[h * nx + x], rr_s.at[slot], dev(me_b, h, x)))
+        gmain[h] = sum(
+            nt(g_hi, m_hi[a, :width]) + nt(g_lo, m_hi[a, :width]) + nt(g_hi, m_lo[a, :width])
+            for a, (g_hi, g_lo) in enumerate(halves))
+        if kh < na - 1:
+            sent.append(send(gmain.at[h], mrecv.at[me_a], ms_s.at[h], mr_s.at[me_a], dev(me_b, h, me_x)))
     rbuf[me_x * na + me_a] = rsend[me_a, :ROWS]
 
     stores = [pltpu.make_async_copy(res, res_out, out_s.at[elems])]
@@ -407,6 +414,22 @@
         copy.wait()
 
 
+def hand_over(new, missed, new_out, missed_out, new_v, missed_v, in_s, out_s):
+    elems = new.shape[0]
+    legs = [(new.at[f], new_v.at[f], new_out.at[f]) for f in range(elems)]
+    legs.append((missed, missed_v, missed_out))
+    ins, outs = [], []
+    for i, (src, mid, dst) in enumerate(legs):
+        ins.append(pltpu.make_async_copy(src, mid, in_s.at[i]))
+        outs.append(pltpu.make_async_copy(mid, dst, out_s.at[i]))
+        ins[-1].start()
+    for arrived, leaving in zip(ins, outs):
+        arrived.wait()
+        leaving.start()
+    for leaving in outs:
+        leaving.wait()
+
+
 def local(sizes, density, measured, offsets, sides, shear_frac, k_incident, k_fluor):
     nb, na, nx = sizes
     elems, slices, cells, width = density.shape
@@ -416,7 +439,7 @@
     rows_h = elems * unit
     hbm = pl.BlockSpec(memory_space=pl.ANY)
     dma = pltpu.SemaphoreType.DMA
-    return pl.pallas_call(
+    new, missed = pl.pallas_call(
         functools.partial(kernel, sizes),
         out_shape=(
             jax.ShapeDtypeStruct((elems, share, cells, width), F32),
@@ -462,6 +485,15 @@
             collective_id=0, has_side_effects=True, vmem_limit_bytes=64 * 1024 * 1024
         ),
     )(density, measured, offsets, sides, shear_frac, k_incident, k_fluor)
+    return pl.pallas_call(
+        hand_over,
+        out_shape=(jax.ShapeDtypeStruct(new.shape, F32), jax.ShapeDtypeStruct(missed.shape, F32)),
+        in_specs=[hbm] * 2,
+        out_specs=(hbm, hbm),
+        scratch_shapes=[pltpu.VMEM(new.shape, F32), pltpu.VMEM(missed.shape, F32),
+                        dma((elems + 1,)), dma((elems + 1,))],
+        compiler_params=pltpu.CompilerParams(vmem_limit_bytes=64 * 1024 * 1024),
+    )(new, missed)
 
 
 def solution(mesh):

time: 25 us -> 23.6 us (0.944)
  local copies, waits for them, and re-layouts: 2.3 us -> 0 us
  Pallas kernels: 21.9 us -> 22.8 us
    unnamed x4 -> x0, local copies, waits for them, and re-layouts: 2.3 us -> none
    pallas_call x0 -> x1, Pallas kernels: none -> 1.66 us  [local(): pl.pallas_call(hand_over, out_shape=(jax.ShapeDtypeStruct(new.shape, F32)...]
    pallas_call x1, Pallas kernels: 21.9 us -> 21.2 us  [local(): pl.pallas_call(functools.partial(kernel, sizes), out_shape=(jax.ShapeDtyp...]
where the time goes in v2:
time: 23.6 us; the launch traced here: 23.5 us
  Pallas kernels  22.8 us (97%)
  between operations  0.64 us (3%)
    pallas_call x1, Pallas kernels, local(): pl.pallas_call(functools.partial(kernel, sizes), out_shape=(jax.ShapeDtyp...  21.2 us
    pallas_call x1, Pallas kernels, local(): pl.pallas_call(hand_over, out_shape=(jax.ShapeDtypeStruct(new.shape, F32)...  1.66 us

profile of v2, /device:TPU:0, one launch (start us, length us, event | category | flops | bytes accessed | tf_op | source)
XLA Modules:
  0.0 23.5 jit_solution(8910570732408103344)
XLA Ops:
  0.6 21.2 %shard_map.86 = (f32[4,2,32,256]{3,2,1,0:T(8,128)}, f32[2,4,4,256]{3,2,1,0:T(4,128)}) custom-call(f32[4,4,32,256]{3,2,1,0:T(8,128)} %dens_in.1, f32[2,4,4,256]{3,2,1,0:T(4,128)} %meas_in.1, s32[2]{0:T(128)} %offs_in.1, s32[2]{0:T(128)} %sides_in.1, f32[2]{0:T(128)} %fracs_in.1, f32[4]{0:T(128)} %kinc_in.1, f32[4,4]{1,0:T(4,128)} %kfl_in.1), custom_call_target="tpu_custom_call" | custom-call | tf_op jit(solution)/shard_map/pallas_call | solution.py:442
  21.8 1.7 %shard_map.87 = (f32[4,2,32,256]{3,2,1,0:T(8,128)}, f32[2,4,4,256]{3,2,1,0:T(4,128)}) custom-call(f32[4,2,32,256]{3,2,1,0:T(8,128)} %get-tuple-element.4.new, f32[2,4,4,256]{3,2,1,0:T(4,128)} %get-tuple-element.5.missed), custom_call_target="tpu_custom_call" | custom-call | tf_op jit(solution)/shard_map/pallas_call | solution.py:488
